TPU v7x, 32 devices: a whole 2x2x4 slice. The times are simulated.
32 devices in a mesh: curve: 8 (over y, x, core), slab: 4 (over z).
Axes of the slice: x: 2, y: 2, z: 4, core: 2. Of those that a mesh axis runs over, the one named last changes fastest.
Arguments:
- start_state: float32 [135, 4096], P(None, ('curve', 'slab')), may hold values from -6 to 6
- right_side: float32 [135, 4096], P(None, ('curve', 'slab')), may hold values from -6 to 6
- block_inverse: float32 [135, 135, 4096], P(None, None, ('curve', 'slab')), as said below
- lifted_flux_jacobian: float32 [6, 135, 45], replicated, may hold values from -0.875 to 0.875
- face_weight: float32 [6, 4096], P(None, ('curve', 'slab')), may hold values from 0.1 to 0.4
- dep_level: int32 [4096], P(('curve', 'slab')), may hold values from 0 to 7
- face_link: int32 [6, 4096], P(None, ('curve', 'slab')), may hold values from -1 to 127, as said below
- send_list: int32 [8, 4096], P(None, ('curve', 'slab')), may hold values from 0 to 768, as said below
- recv_list: int32 [8, 4096], P(None, ('curve', 'slab')), may hold values from 0 to 768, as said below
Outputs:
- forward_state: float32 [135, 4096], P(None, ('curve', 'slab'))
- swept_state: float32 [135, 4096], P(None, ('curve', 'slab'))
Inputs may be any that keep to these rules, and one draw needn't show every extreme that they name: `block_inverse`: A dense 135 x 135 matrix for each element. `face_link`: for face d of element k of a device, the index on the same device of the element across that face, or -1 where that element lies on another device or outside the domain; links are mutual. `send_list`: A device's shard holds, for each level, 4 slots for each destination device in order; an entry d * 128 + k names face d of the device's local element k, and 768 marks an empty slot. Non-empty slots go only to devices whose curve index differs from the sender's by at most one. In every draw some device fills all 4 slots to one destination at every level. `recv_list`: A device's shard holds, for each level, 4 slots for each source device in order; slot j from source t names the face index at which t's slot j toward this device arrives, empty (768) exactly where that send slot is empty. Over all levels no face appears twice in one device's shard. Non-empty slots come only from devices whose curve index differs by at most one.
All inputs are finite; a program needn't handle non-finite values.
Results may differ from a plain program's by a relative error of at most 0.0003.
Values sent between devices are 32-bit elements; how exact they have to be, the bound alone decides.
No kernel may reach another device: no remote copies, remote signals or barrier semaphores. Data moves between devices by JAX's collectives and lax.ppermute only.
A program may use at most 64 MiB of HBM per device.

v0:
```python
import functools

import jax
import jax.numpy as jnp
import numpy as np
from jax import lax
from jax.experimental import pallas as pl
from jax.experimental.pallas import tpu as pltpu
from jax.sharding import PartitionSpec as P

VARS = 5
SIDE = 3
FACES = 6
LANES = 128
SUB = 8
GROUPS = 8
F32 = jnp.float32
BF16 = jnp.bfloat16


class Sizes:
    def __init__(self, block, columns, levels, slots, curves, slabs):
        self.block = block
        self.columns = columns
        self.levels = levels
        self.slots = slots
        self.curves = curves
        self.slabs = slabs
        self.devices = curves * slabs
        self.trace = VARS * SIDE * SIDE
        self.width = columns // GROUPS
        self.rows = -(-block // GROUPS)
        self.rows_pad = -(-(self.rows + 1) // SUB) * SUB
        self.state_rows = GROUPS * self.rows_pad
        self.block_pad = -(-block // SUB) * SUB
        self.flag = self.trace
        self.wish = self.trace + 1
        self.trace_pad = -(-(self.trace + 2) // 16) * 16
        self.cuts = self.trace_pad // 16
        self.table_rows = FACES * self.trace_pad
        self.jac_rows = -(-self.block_pad // 16) * 16
        assert columns == LANES and slabs * slots == LANES
        assert (self.cuts + 1) * slots <= LANES and block < self.block_pad


def face_rows():
    nodes = np.arange(VARS * SIDE**3).reshape(VARS, SIDE, SIDE, SIDE)
    last = SIDE - 1
    sides = [
        nodes[:, 0],
        nodes[:, last],
        nodes[:, :, 0],
        nodes[:, :, last],
        nodes[:, :, :, 0],
        nodes[:, :, :, last],
    ]
    return [side.reshape(-1) for side in sides]


def selector(z):
    pick = np.zeros((z.table_rows, z.state_rows), np.float32)
    for face, rows in enumerate(face_rows()):
        for h, i in enumerate(rows):
            pick[face * z.trace_pad + h, i // z.rows * z.rows_pad + i % z.rows] = 1
        pick[face * z.trace_pad + z.flag, z.rows] = 1
    return np.concatenate([pick, pick], axis=1)


def lane_take(values, index):
    index = jnp.broadcast_to(index, values.shape)
    return jnp.take_along_axis(values, index, axis=1, mode="promise_in_bounds")


def lane_iota(rows=SUB):
    return lax.broadcasted_iota(jnp.int32, (rows, LANES), 1)


def halves(values):
    high = values.astype(BF16)
    low = (values - high.astype(F32)).astype(BF16)
    return high, low


def as_column(row):
    return jnp.broadcast_to(row, (LANES, LANES)).T


def dot(a, b):
    return jnp.dot(a, b, preferred_element_type=F32)


def tables_of(state, pick):
    high, low = halves(state)
    return dot(pick, jnp.concatenate([high, low], axis=0))


def fluxes(jac, traces):
    high, low = halves(traces)
    return dot(jac, jnp.concatenate([high, low, high], axis=0))


def pack(z, message, group, curve, open_sends, out_ref):
    lanes = lane_iota(16)
    target = curve + group - 1

    @pl.when((target >= 0) & (target < z.curves))
    def _():
        for slab in range(z.slabs):
            block = jnp.broadcast_to(open_sends, (16, LANES))
            for cut in range(z.cuts):
                part = message[cut * 16 : cut * 16 + 16]
                shift = (cut - slab) * z.slots % LANES
                part = pltpu.roll(part, shift, 1) if shift else part
                block = jnp.where(lanes // z.slots == cut, part, block)
            out_ref[target * z.slabs + slab] = block


def unpack(z, group, curve, in_ref):
    lanes = lane_iota(16)
    source = jnp.clip(curve + group - 1, 0, z.curves - 1)
    blocks = [in_ref[source * z.slabs + slab] for slab in range(z.slabs)]
    parts = []
    for cut in range(z.cuts):
        part = jnp.zeros((16, LANES), F32)
        for slab in range(z.slabs):
            shift = (slab - cut) * z.slots % LANES
            block = pltpu.roll(blocks[slab], shift, 1) if shift else blocks[slab]
            part = jnp.where(lanes // z.slots == slab, block, part)
        parts.append(part)
    return jnp.concatenate(parts, axis=0)


def ghost_take(z, slot_traces, where, face):
    index = jnp.maximum(where[face : face + 1], 0)
    lane = jnp.bitwise_and(index, LANES - 1)
    block = index // LANES
    found = jnp.zeros((z.trace_pad, LANES), F32)
    for group in range(3):
        found = jnp.where(block == group, lane_take(slot_traces[group], lane), found)
    return found


def regroup(z, lists_ref, level_ref):
    n = z.columns
    cap = z.slots // z.levels
    lane = lane_iota(1)
    source = lane // z.slots * cap + jnp.bitwise_and(lane, cap - 1)
    row_id = lax.broadcasted_iota(jnp.int32, (z.levels, n), 0)
    own_row = row_id == level_ref[...]
    both = []
    for at in range(2):
        lists = lists_ref[pl.ds(at * z.levels, z.levels), :]
        rows = []
        for group in range(3):
            taken = lane_take(lists, source + group * z.slabs * cap)
            rows.append(jnp.sum(jnp.where(own_row, taken, 0).astype(F32), axis=0, keepdims=True))
        rows.append(jnp.full((SUB - 3, n), float(FACES * n), F32))
        both.append(jnp.concatenate(rows, axis=0).astype(jnp.int32))
    return both


def prepare_kernel(
    z,
    curve_ref,
    start_ref,
    dep_ref,
    link_ref,
    weight_ref,
    lists_ref,
    level_ref,
    pick_ref,
    ints_ref,
    floats_ref,
    sends_ref,
    span_ref,
    table_ref,
    message_ref,
    state_ref,
):
    n = z.columns
    lanes = lane_iota()
    dep_row = dep_ref[...]
    dep = jnp.broadcast_to(dep_row, (SUB, n))
    key = (dep_row * n + lane_iota(1)).astype(F32)
    earlier = as_column(key) < jnp.broadcast_to(key, (n, n))
    pos_row = jnp.sum(jnp.where(earlier, 1.0, 0.0), axis=0, keepdims=True)
    here = as_column(pos_row) == lane_iota(n).astype(F32)
    element = lax.broadcasted_iota(jnp.int32, (n, n), 0).astype(F32)
    perm_row = jnp.sum(jnp.where(here, element, 0.0), axis=0, keepdims=True)
    pos = jnp.broadcast_to(pos_row.astype(jnp.int32), (SUB, n))
    perm = jnp.broadcast_to(perm_row.astype(jnp.int32), (SUB, n))
    dep_sorted = lane_take(dep, perm)
    for level in range(z.levels):
        before = jnp.sum(jnp.where(dep_row < level, 1.0, 0.0)).astype(jnp.int32)
        upto = jnp.sum(jnp.where(dep_row <= level, 1.0, 0.0)).astype(jnp.int32)
        span_ref[level] = before // z.width
        span_ref[z.levels + level] = jnp.where(upto > before, (upto + z.width - 1) // z.width, before // z.width)

    link = jnp.concatenate([link_ref[...], jnp.full((SUB - FACES, n), -1, jnp.int32)], axis=0)
    near = jnp.where(link >= 0, lane_take(pos, jnp.maximum(link, 0)), -1)
    near = lane_take(near, perm)
    weight = jnp.concatenate([weight_ref[...], jnp.zeros((SUB - FACES, n), F32)], axis=0)
    weight = lane_take(weight, perm)
    local = near >= 0
    near = jnp.maximum(near, 0)
    dep_near = lane_take(dep_sorted, near)
    zero = jnp.zeros_like(weight)

    send, recv = regroup(z, lists_ref, level_ref)
    slot_level = jnp.broadcast_to(level_ref[...], (SUB, n))
    rows = []
    slot_id = lax.broadcasted_iota(jnp.int32, (n, n), 0).astype(F32) + 1.0
    columns = [as_column(recv[group : group + 1].astype(F32)) for group in range(3)]
    for face in range(FACES):
        name = (lane_iota(n) + face * n).astype(F32)
        found = jnp.zeros((1, n), F32)
        for group in range(3):
            hit = jnp.where(columns[group] == name, slot_id + float(group * n), 0.0)
            found = jnp.maximum(found, jnp.max(hit, axis=0, keepdims=True))
        rows.append(found)
    rows.append(jnp.zeros((SUB - FACES, n), F32))
    slot = jnp.concatenate(rows, axis=0).astype(jnp.int32) - 1
    slot = lane_take(slot, perm)
    from_far = slot >= 0
    slot = jnp.maximum(slot, 0)
    far_level = lane_take(slot_level, jnp.bitwise_and(slot, n - 1))

    for at, value in enumerate((pos, perm, dep_sorted, near, slot)):
        ints_ref[at] = value
    floats_ref[0] = jnp.where(local & (dep_near < dep_sorted), weight, zero)
    floats_ref[1] = jnp.where(local & (dep_near > dep_sorted), weight, zero)
    floats_ref[2] = jnp.where(local & (dep_near <= dep_sorted), weight, zero)
    floats_ref[3] = jnp.where(local & (dep_near >= dep_sorted), weight, zero)
    floats_ref[4] = jnp.where(from_far & (far_level < dep_sorted), weight, zero)
    floats_ref[5] = jnp.where(from_far, weight, zero)
    floats_ref[6] = jnp.where(from_far & (far_level >= dep_sorted), weight, zero)

    send_element = jnp.bitwise_and(send, n - 1)
    sends_ref[0] = lane_take(pos, send_element)
    sends_ref[1] = send // n
    sends_ref[2] = lane_take(dep, send_element)
    recv_dep = lane_take(dep, jnp.bitwise_and(recv, n - 1))
    wish = jnp.where(slot_level <= recv_dep, 1.0, 0.0)

    state_ref[...] = jnp.zeros_like(state_ref)
    for group in range(GROUPS):
        count = min(z.rows, z.block - group * z.rows)
        state_ref[pl.ds(group * z.rows_pad, count), :] = start_ref[pl.ds(group * z.rows, count), :]
    state_ref[pl.ds(z.rows, 1), :] = jnp.ones((1, n), F32)
    state = lane_take(state_ref[...], perm[0:1])
    table = tables_of(state, pick_ref[...])
    table_ref[...] = table
    message_ref[...] = jnp.zeros_like(message_ref)
    row_id = lax.broadcasted_iota(jnp.int32, (z.trace_pad, n), 0)
    for group in range(3):
        where = sends_ref[0][group : group + 1]
        side = sends_ref[1][group : group + 1]
        message = jnp.zeros((z.trace_pad, n), F32)
        for face in range(FACES):
            piece = table[face * z.trace_pad : (face + 1) * z.trace_pad]
            message = jnp.where(side == face, lane_take(piece, where), message)
        message = jnp.where(row_id == z.wish, wish[group : group + 1], message)
        pack(z, message, group, curve_ref[0], jnp.zeros((1, n), F32), message_ref)


def block_copies(z, ii, inverse_ref, buffer_ref, sems):
    slot = lax.rem(ii, buffer_ref.shape[0])
    for group in range(GROUPS):
        i = jnp.minimum(group * z.rows + ii, z.block - 1)
        yield pltpu.make_async_copy(
            inverse_ref.at[i], buffer_ref.at[slot, group, pl.ds(0, z.block)], sems.at[slot, group]
        )


def chunk_tables(z, ints_ref, floats_ref, near_ref, weights_ref):
    for chunk in range(GROUPS):
        own = chunk * z.width + jnp.bitwise_and(lane_iota(), z.width - 1)
        near_ref[chunk] = lane_take(ints_ref[3], own)
        for at in range(3):
            weights_ref[chunk, at] = lane_take(floats_ref[at], own)


def chunk_copy(ii, chunks_ref, out_ref, sems):
    return pltpu.make_async_copy(chunks_ref.at[:, ii], out_ref.at[:, ii], sems.at[ii])


def arrange_blocks(z, inverse_ref, ints_ref, chunks_ref, out_ref, buffer_ref, sems, out_sems):
    n = z.columns
    perm = ints_ref[1]
    depth = buffer_ref.shape[0]
    orders = [pltpu.roll(perm, group * z.width, 1) if group else perm for group in range(GROUPS)]
    bits = [jnp.bitwise_and(lane_iota() // (z.width << b), 1) == 1 for b in range(3)]

    def row(ii, carry):
        @pl.when(ii + depth - 1 < z.rows)
        def _():
            for copy in block_copies(z, ii + depth - 1, inverse_ref, buffer_ref, sems):
                copy.start()

        for copy in block_copies(z, ii, inverse_ref, buffer_ref, sems):
            copy.wait()
        slot = lax.rem(ii, depth)
        for tile in range(z.block_pad // SUB):
            at = pl.ds(tile * SUB, SUB)
            spread = [lane_take(buffer_ref[slot, group, at, :], orders[group]) for group in range(GROUPS)]
            for b in range(3):
                spread = [
                    jnp.where(bits[b], spread[(x + (1 << b)) % GROUPS], spread[x])
                    for x in range(GROUPS)
                ]
            for chunk in range(GROUPS):
                chunks_ref[chunk, ii, at, :] = spread[-chunk % GROUPS]
        chunk_copy(ii, chunks_ref, out_ref, out_sems).start()
        return carry

    lax.fori_loop(0, z.rows, row, 0)


def first_base(z, traces, start_table_ref, ints_ref, floats_ref, right_ref, jac_ref, stack_ref, right_sorted_ref, base_ref):
    n = z.columns
    near = ints_ref[3]
    slot = ints_ref[4]
    for face in range(FACES):
        piece = start_table_ref[pl.ds((face ^ 1) * z.trace_pad, z.trace_pad), :]
        value = lane_take(piece, near[face : face + 1]) * floats_ref[3][face : face + 1]
        ghost = ghost_take(z, traces, slot, face) * floats_ref[6][face : face + 1]
        stack_ref[pl.ds(face * z.trace_pad, z.trace_pad), :] = value + ghost
    flow = fluxes(jac_ref[...], stack_ref[...])[: z.block_pad]
    right = jnp.concatenate([right_ref[...], jnp.zeros((z.block_pad - z.block, n), F32)], axis=0)
    right = lane_take(right, ints_ref[1][0:1])
    right_sorted_ref[...] = right
    base_ref[...] = right - flow


def send_kinds(z, traces, sends_ref, level_ref, kinds_ref):
    for group in range(3):
        wish = traces[group][z.wish : z.wish + 1] > 0.5
        side = sends_ref[1][group : group + 1]
        dep = sends_ref[2][group : group + 1]
        level = level_ref[...]
        kind = jnp.where(wish, jnp.where(dep <= level, 1, 3), jnp.where(dep >= level, 2, 1))
        kinds_ref[pl.ds(group, 1), :] = jnp.where(side < FACES, kind, 0)


def later_bases(z, traces, ints_ref, floats_ref, base_ref, right_ref, jac_ref, wide_ref, forward_base_ref, swept_base_ref):
    n = z.columns
    slot = ints_ref[4]
    missing_forward = jnp.zeros((1, n), F32)
    missing_swept = jnp.zeros((1, n), F32)
    for face in range(FACES):
        ghost = ghost_take(z, traces, slot, face)
        forward_weight = floats_ref[4][face : face + 1]
        swept_weight = floats_ref[5][face : face + 1]
        lost = jnp.where(ghost[z.flag : z.flag + 1] > 0.5, 0.0, 1.0)
        missing_forward += jnp.where(forward_weight > 0, lost, 0.0)
        missing_swept += jnp.where(swept_weight > 0, lost, 0.0)
        at = pl.ds(face * z.trace_pad, z.trace_pad)
        wide_ref[at, pl.ds(0, n)] = ghost * forward_weight
        wide_ref[at, pl.ds(n, n)] = ghost * swept_weight
    flow = fluxes(jac_ref[...], wide_ref[...])
    forward_base_ref[...] = base_ref[...] - flow[: z.block_pad, :n]
    swept_base_ref[...] = right_ref[...] - flow[: z.block_pad, n:]
    return missing_forward, missing_swept


def steps(
    z,
    span_ref,
    missing_forward,
    missing_swept,
    ints_ref,
    floats_ref,
    near_ref,
    weights_ref,
    jac_ref,
    pick_ref,
    chunks_ref,
    forward_table_ref,
    swept_table_ref,
    forward_ref,
    swept_ref,
    forward_base,
    swept_base,
    stack_ref,
    part_ref,
    fresh_ref,
    fetches,
):
    n = z.columns
    near = ints_ref[3]
    dep = ints_ref[2]
    chunk_of = lane_iota(1) // z.width
    per_sum = GROUPS // 2
    part_ref[...] = jnp.where(
        lax.broadcasted_iota(jnp.int32, (z.rows_pad, n), 0) == z.rows, 1.0, 0.0
    )

    def spread(row):
        return jnp.broadcast_to(row, (SUB, n))

    def absent(flags, weights):
        lost = jnp.where(weights > 0, 1.0 - lane_take(flags, near), 0.0)
        return jnp.sum(lost, axis=0, keepdims=True)

    old_forward = spread(forward_table_ref[pl.ds(z.flag, 1), :])
    old_swept = spread(swept_table_ref[pl.ds(z.flag, 1), :])
    forward, swept = old_forward, old_swept
    for level in range(z.levels):
        missing = absent(forward, floats_ref[0]) + missing_forward
        forward = jnp.where((dep == level) & spread(missing < 0.5), 1.0, forward)
    settled = absent(forward, floats_ref[2]) + missing_swept
    for level in range(z.levels - 1, -1, -1):
        missing = absent(swept, floats_ref[1]) + settled
        swept = jnp.where((dep == level) & spread(missing < 0.5), 1.0, swept)
    counts = []
    for at, fresh in enumerate((forward - old_forward, swept - old_swept)):
        fresh = fresh[0:1]
        fresh_ref[pl.ds(at, 1), :] = fresh
        for half in range(2):
            scale = jnp.zeros((1, n), F32)
            for at_chunk in range(per_sum):
                scale = jnp.where(chunk_of == half * per_sum + at_chunk, float((2 * z.width) ** at_chunk), scale)
            counts.append(jnp.sum(fresh * scale).astype(jnp.int32))

    for fetch in fetches:
        fetch.wait()

    def step(level, chunk, backward):
        old = forward_table_ref
        new = swept_table_ref
        base = swept_base if backward else forward_base
        rows = near_ref[chunk]
        old_weight = weights_ref[chunk, 2 if backward else 0]
        new_weight = weights_ref[chunk, 1]
        own = chunk * z.width + jnp.bitwise_and(lane_iota(1), z.width - 1)
        for face in range(FACES):
            at = pl.ds((face ^ 1) * z.trace_pad, z.trace_pad)
            row = rows[face : face + 1]
            value = lane_take(old[at, :], row) * old_weight[face : face + 1]
            if backward:
                value += lane_take(new[at, :], row) * new_weight[face : face + 1]
            stack_ref[pl.ds(face * z.trace_pad, z.trace_pad), :] = value
        flow = fluxes(jac_ref[...], stack_ref[...])[: z.block_pad]
        rest = lane_take(base[...], own) - flow
        for ii in range(z.rows):
            part_ref[pl.ds(ii, 1), :] = jnp.sum(chunks_ref[chunk, ii] * rest, axis=0, keepdims=True)
        part = part_ref[...]
        state = jnp.concatenate(
            [pltpu.roll(part, -g * z.width % n, 1) if g else part for g in range(GROUPS)], axis=0
        )
        table = tables_of(state, pick_ref[...])
        fresh = fresh_ref[pl.ds(1 if backward else 0, 1), :] > 0.5
        keep = fresh & (chunk_of == chunk) & (dep[0:1] == level)
        out_state = swept_ref if backward else forward_ref
        out_table = swept_table_ref if backward else forward_table_ref
        out_state[...] = jnp.where(keep, state, out_state[...])
        out_table[...] = jnp.where(keep, table, out_table[...])

    for backward in (False, True):
        low, high = counts[2 * backward], counts[2 * backward + 1]

        def run(count, carry, backward=backward, low=low, high=high):
            level = z.levels - 1 - count if backward else count

            def one(chunk, inner):
                bits = jnp.where(chunk >= per_sum, high, low)
                shift = (2 * z.width).bit_length() - 1
                bits = lax.shift_right_logical(bits, lax.rem(chunk, per_sum) * shift)

                @pl.when(jnp.bitwise_and(bits, 2 * z.width - 1) > 0)
                def _():
                    step(level, chunk, backward)

                return inner

            return lax.fori_loop(span_ref[level], span_ref[z.levels + level], one, carry)

        lax.fori_loop(0, z.levels, run, 0)


def send_messages(z, curve, sends_ref, kinds_ref, forward_table_ref, swept_table_ref, message_ref):
    n = z.columns
    row_id = lax.broadcasted_iota(jnp.int32, (z.trace_pad, n), 0)
    messages = []
    still = jnp.zeros((1, n), F32)
    for group in range(3):
        where = sends_ref[0][group : group + 1]
        side = sends_ref[1][group : group + 1]
        kind = kinds_ref[pl.ds(group, 1), :]
        message = jnp.zeros((z.trace_pad, n), F32)
        for face in range(FACES):
            at = pl.ds(face * z.trace_pad, z.trace_pad)
            first = lane_take(forward_table_ref[at, :], where)
            second = lane_take(swept_table_ref[at, :], where)
            picked = jnp.where(kind == 1, first, second)
            message = jnp.where(side == face, picked, message)
        message = jnp.where((kind == 3) & (row_id == z.flag), 2.0, message)
        unsent = (kind > 0) & (message[z.flag : z.flag + 1] < 0.5)
        still = jnp.maximum(still, jnp.where(unsent, 1.0, 0.0))
        messages.append(message)
    still = jnp.broadcast_to(jnp.max(still, axis=1, keepdims=True), (1, n))
    message_ref[...] = jnp.broadcast_to(still[None], message_ref.shape)
    for group in range(3):
        pack(z, messages[group], group, curve, still, message_ref)


def first_kernel(
    z,
    curve_ref,
    span_ref,
    right_ref,
    level_ref,
    start_table_ref,
    arrived_ref,
    ints_ref,
    floats_ref,
    sends_ref,
    jac_ref,
    pick_ref,
    inverse_ref,
    message_ref,
    base_ref,
    right_sorted_ref,
    start_slots_ref,
    kinds_ref,
    chunks_out,
    near_ref,
    weights_ref,
    forward_table_ref,
    swept_table_ref,
    forward_ref,
    swept_ref,
    stack_ref,
    part_ref,
    fresh_ref,
    buffer_ref,
    chunks_ref,
    sems,
    out_sems,
):
    n = z.columns
    curve = curve_ref[0]
    depth = buffer_ref.shape[0]
    buffer_ref[:, :, z.block :, :] = jnp.zeros((depth, GROUPS, z.block_pad - z.block, n), F32)
    for first in range(depth - 1):
        for copy in block_copies(z, first, inverse_ref, buffer_ref, sems):
            copy.start()
    chunk_tables(z, ints_ref, floats_ref, near_ref, weights_ref)
    traces = [unpack(z, group, curve, arrived_ref) for group in range(3)]
    for group in range(3):
        start_slots_ref[group] = traces[group]
    send_kinds(z, traces, sends_ref, level_ref, kinds_ref)
    first_base(
        z, traces, start_table_ref, ints_ref, floats_ref, right_ref, jac_ref, stack_ref, right_sorted_ref, base_ref
    )
    forward_table_ref[...] = jnp.zeros_like(forward_table_ref)
    swept_table_ref[...] = jnp.zeros_like(swept_table_ref)
    forward_ref[...] = jnp.zeros_like(forward_ref)
    swept_ref[...] = jnp.zeros_like(swept_ref)
    arrange_blocks(z, inverse_ref, ints_ref, chunks_ref, chunks_out, buffer_ref, sems, out_sems)
    missing_forward = jnp.sum(jnp.where(floats_ref[4] > 0, 1.0, 0.0), axis=0, keepdims=True)
    missing_swept = jnp.sum(jnp.where(floats_ref[5] > 0, 1.0, 0.0), axis=0, keepdims=True)
    steps(
        z,
        span_ref,
        missing_forward,
        missing_swept,
        ints_ref,
        floats_ref,
        near_ref,
        weights_ref,
        jac_ref,
        pick_ref,
        chunks_ref,
        forward_table_ref,
        swept_table_ref,
        forward_ref,
        swept_ref,
        base_ref,
        right_sorted_ref,
        stack_ref,
        part_ref,
        fresh_ref,
        (),
    )
    send_messages(z, curve, sends_ref, kinds_ref, forward_table_ref, swept_table_ref, message_ref)
    for ii in range(z.rows):
        chunk_copy(ii, chunks_ref, chunks_out, out_sems).wait()


def round_kernel(
    z,
    curve_ref,
    span_ref,
    arrived_ref,
    ints_ref,
    floats_ref,
    sends_ref,
    near_ref,
    weights_ref,
    jac_ref,
    pick_ref,
    chunks_in,
    base_ref,
    right_ref,
    start_slots_ref,
    kinds_ref,
    forward_table_in,
    swept_table_in,
    forward_in,
    swept_in,
    message_ref,
    more_ref,
    forward_table_ref,
    swept_table_ref,
    forward_ref,
    swept_ref,
    stack_ref,
    part_ref,
    fresh_ref,
    wide_ref,
    forward_base_ref,
    swept_base_ref,
    chunks_ref,
    sems,
):
    n = z.columns
    curve = curve_ref[0]
    fetches = [
        pltpu.make_async_copy(chunks_in.at[chunk], chunks_ref.at[chunk], sems.at[chunk]) for chunk in range(GROUPS)
    ]
    for fetch in fetches:
        fetch.start()
    forward_table_ref[...] = forward_table_in[...]
    swept_table_ref[...] = swept_table_in[...]
    forward_ref[...] = forward_in[...]
    swept_ref[...] = swept_in[...]
    row_id = lax.broadcasted_iota(jnp.int32, (z.trace_pad, n), 0)
    still = jnp.max(arrived_ref[:, 0:1, :], axis=0)
    still = jnp.where(lane_iota(1) == n - 1, still, 0.0)
    more_ref[0] = jnp.max(still).astype(jnp.int32)
    traces = []
    for group in range(3):
        arrived = unpack(z, group, curve, arrived_ref)
        flag = arrived[z.flag : z.flag + 1]
        traces.append(jnp.where((flag > 1.5) & (row_id != z.flag), start_slots_ref[group], arrived))
    missing_forward, missing_swept = later_bases(
        z, traces, ints_ref, floats_ref, base_ref, right_ref, jac_ref, wide_ref, forward_base_ref, swept_base_ref
    )
    steps(
        z,
        span_ref,
        missing_forward,
        missing_swept,
        ints_ref,
        floats_ref,
        near_ref,
        weights_ref,
        jac_ref,
        pick_ref,
        chunks_ref,
        forward_table_ref,
        swept_table_ref,
        forward_ref,
        swept_ref,
        forward_base_ref,
        swept_base_ref,
        stack_ref,
        part_ref,
        fresh_ref,
        fetches,
    )
    send_messages(z, curve, sends_ref, kinds_ref, forward_table_ref, swept_table_ref, message_ref)


def output_kernel(z, ints_ref, forward_ref, swept_ref, forward_out, swept_out):
    pos = ints_ref[0][0:1]
    for source, target in ((forward_ref, forward_out), (swept_ref, swept_out)):
        for group in range(GROUPS):
            count = min(z.rows, z.block - group * z.rows)
            block = lane_take(source[pl.ds(group * z.rows_pad, z.rows_pad), :], pos)
            target[pl.ds(group * z.rows, count), :] = block[:count]


def call(kernel, outs, inputs, scratch=(), aliases=None, smem_in=(), smem_out=(), hbm_in=(), hbm_out=(), vmem=24):
    whole, smem = pl.BlockSpec(memory_space=pltpu.VMEM), pl.BlockSpec(memory_space=pltpu.SMEM)
    hbm = pl.BlockSpec(memory_space=pltpu.HBM)
    return pl.pallas_call(
        kernel,
        out_shape=outs,
        in_specs=[smem if at in smem_in else hbm if at in hbm_in else whole for at in range(inputs)],
        out_specs=[smem if at in smem_out else hbm if at in hbm_out else whole for at in range(len(outs))],
        scratch_shapes=list(scratch),
        input_output_aliases=aliases or {},
        compiler_params=pltpu.CompilerParams(vmem_limit_bytes=vmem << 20),
    )


def shape(*dims, kind=F32):
    return jax.ShapeDtypeStruct(dims, kind)


def kept(*dims, kind=F32):
    return pltpu.VMEM(dims, kind)


def body(
    start_state,
    right_side,
    block_inverse,
    lifted_flux_jacobian,
    face_weight,
    dep_level,
    face_link,
    send_list,
    recv_list,
):
    curves, slabs = lax.axis_size("curve"), lax.axis_size("slab")
    levels = send_list.shape[0]
    cap = send_list.shape[1] // (curves * slabs)
    slots = levels * cap
    block, n = start_state.shape
    z = Sizes(block, n, levels, slots, curves, slabs)
    own = lax.axis_index("curve").astype(jnp.int32)
    curve = own.reshape(1)

    stride = slabs * cap
    lists = jnp.concatenate([send_list, recv_list], axis=0)
    lists = jnp.pad(lists, ((0, 0), (stride, n)), constant_values=FACES * n)
    lists = lax.dynamic_slice_in_dim(lists, own * stride, n, axis=1)
    slot_level = jnp.asarray(
        np.tile(np.repeat(np.arange(levels), cap), slabs).reshape(1, n), jnp.int32
    )
    pick = jnp.asarray(selector(z), BF16)
    jac = jnp.pad(
        lifted_flux_jacobian, ((0, 0), (0, z.jac_rows - block), (0, z.trace_pad - z.trace))
    )
    jac = jac.transpose(1, 0, 2).reshape(z.jac_rows, z.table_rows)
    rounded = lax.reduce_precision(jac, 8, 7)
    high, low = rounded.astype(BF16), (jac - rounded).astype(BF16)
    jac = jnp.concatenate([high, high, low], axis=1)

    ints, floats, sends, span, start_table, message = call(
        functools.partial(prepare_kernel, z),
        [
            kept(5, SUB, n, kind=jnp.int32),
            kept(7, SUB, n),
            kept(3, SUB, n, kind=jnp.int32),
            shape(2 * levels, kind=jnp.int32),
            kept(z.table_rows, n),
            shape(z.devices, 16, n),
        ],
        8,
        scratch=[pltpu.VMEM((z.state_rows, n), F32)],
        smem_in=(0,),
        smem_out=(3,),
        vmem=60,
    )(curve, start_state, dep_level.reshape(1, n), face_link, face_weight, lists, slot_level, pick)
    message, jac = lax.optimization_barrier((message, jac))

    def exchange(message):
        return lax.all_to_all(message, ("curve", "slab"), 0, 0, tiled=True)

    arrived = exchange(message)
    tables = [
        kept(z.table_rows, n),
        kept(z.table_rows, n),
        kept(z.state_rows, n),
        kept(z.state_rows, n),
    ]
    scratch = [
        pltpu.VMEM((z.table_rows, n), F32),
        pltpu.VMEM((z.rows_pad, n), F32),
        pltpu.VMEM((SUB, n), F32),
    ]
    depth = 6
    message, base, right, start_slots, kinds, chunks, near, weights, *state = call(
        functools.partial(first_kernel, z),
        [
            shape(z.devices, 16, n),
            kept(z.block_pad, n),
            kept(z.block_pad, n),
            kept(3, z.trace_pad, n),
            kept(3, n, kind=jnp.int32),
            shape(GROUPS, z.rows, z.block_pad, n),
            kept(GROUPS, SUB, n, kind=jnp.int32),
            kept(GROUPS, 3, SUB, n),
        ]
        + tables,
        12,
        scratch=scratch
        + [
            pltpu.VMEM((depth, GROUPS, z.block_pad, n), F32),
            pltpu.VMEM((GROUPS, z.rows, z.block_pad, n), F32),
            pltpu.SemaphoreType.DMA((depth, GROUPS)),
            pltpu.SemaphoreType.DMA((z.rows,)),
        ],
        smem_in=(0, 1),
        hbm_in=(11,),
        hbm_out=(5,),
        vmem=56,
    )(
        curve,
        span,
        right_side,
        slot_level,
        start_table,
        arrived,
        ints,
        floats,
        sends,
        jac,
        pick,
        block_inverse,
    )

    round_call = call(
        functools.partial(round_kernel, z),
        [shape(z.devices, 16, n), shape(1, kind=jnp.int32)] + tables,
        19,
        scratch=scratch
        + [
            pltpu.VMEM((z.table_rows, 2 * n), F32),
            pltpu.VMEM((z.block_pad, n), F32),
            pltpu.VMEM((z.block_pad, n), F32),
            pltpu.VMEM((GROUPS, z.rows, z.block_pad, n), F32),
            pltpu.SemaphoreType.DMA((GROUPS,)),
        ],
        hbm_in=(10,),
        vmem=56,
        aliases={15: 2, 16: 3, 17: 4, 18: 5},
        smem_in=(0, 1),
        smem_out=(1,),
    )

    def one_round(carry):
        _, message, state = carry
        message, more, *state = round_call(
            curve,
            span,
            exchange(message),
            ints,
            floats,
            sends,
            near,
            weights,
            jac,
            pick,
            chunks,
            base,
            right,
            start_slots,
            kinds,
            *state,
        )
        return more[0], message, tuple(state)

    start = (jnp.array(1, jnp.int32), message, tuple(state))
    _, _, state = lax.while_loop(lambda carry: carry[0] > 0, one_round, start)
    return tuple(
        call(functools.partial(output_kernel, z), [shape(block, n), shape(block, n)], 3)(
            ints, state[2], state[3]
        )
    )


def solution(mesh):
    split = ("curve", "slab")
    return jax.shard_map(
        body,
        mesh=mesh,
        in_specs=(
            P(None, split),
            P(None, split),
            P(None, None, split),
            P(),
            P(None, split),
            P(split),
            P(None, split),
            P(None, split),
            P(None, split),
        ),
        out_specs=(P(None, split), P(None, split)),
        check_vma=False,
    )
```

profile of v0, /device:TPU:1, one launch (start us, length us, event | category | flops | bytes accessed | tf_op | source)
XLA Modules:
  0.0 215.3 jit_solution(9736620352848623275)
XLA Ops:
  0.6 1.0 pad.9
  1.9 0.7 pad_add_fusion
  2.6 0.7 pad_dynamic-slice_fusion.lists_ref
  3.2 0.1 pad_maximum_fusion.jac_ref
  3.4 3.1 %shard_map.122 = (s32[5,8,128]{2,1,0:T(8,128)S(1)}, f32[7,8,128]{2,1,0:T(8,128)S(1)}, s32[3,8,128]{2,1,0:T(8,128)S(1)}, s32[16]{0:T(128)S(1)}, f32[288,128]{1,0:T(8,128)S(1)}, /*index=5*/f32[32,16,128]{2,1,0:T(8,128)}) custom-call(s32[1]{0:T(128)} %bitcast.curve_ref, f32[135,128]{1,0:T(8,128)} %start_ref.1, s32[1,128]{1,0:T(1,128)} %bitcast.8, ...), custom_call_target="tpu_custom_call" | custom-call | tf_op jit(solution)/shard_map/pallas_call | solution.py:743
  6.5 0.6 copy-done
  7.1 7.1 %all-to-all-start.1 = ((f32[32,16,128]{2,1,0:T(8,128)}), f32[32,16,128]{2,1,0:T(8,128)S(1)}, u32[]{:S(2)}, u32[]{:S(2)}) async-start(f32[32,16,128]{2,1,0:T(8,128)} %get-tuple-element.134), calls=%async_computation.1 | async-start | bytes 524288 | tf_op jit(solution)/shard_map/all_to_all | solution.py:762
  14.2 10.3 %all-to-all-done.1.arrived_ref = f32[32,16,128]{2,1,0:T(8,128)S(1)} async-done(((f32[32,16,128]{2,1,0:T(8,128)}), f32[32,16,128]{2,1,0:T(8,128)S(1)}, u32[]{:S(2)}, u32[]{:S(2)}) %all-to-all-start.1) | async-done | bytes 262176 | tf_op jit(solution)/shard_map/all_to_all | solution.py:762
  24.6 0.7 copy-done.2
  25.3 24.7 %shard_map.123 = (f32[32,16,128]{2,1,0:T(8,128)S(1)}, f32[136,128]{1,0:T(8,128)S(1)}, f32[136,128]{1,0:T(8,128)S(1)}, f32[3,48,128]{2,1,0:T(8,128)S(1)}, s32[3,1...) custom-call(s32[1]{0:T(128)} %bitcast.curve_ref, ...), custom_call_target="tpu_custom_call" | custom-call | tf_op jit(solution)/shard_map/pallas_call | solution.py:777
  49.9 164.6 %while.19 = (s32[]{:T(128)}, f32[32,16,128]{2,1,0:T(8,128)S(1)}, f32[288,128]{1,0:T(8,128)S(1)}, f32[288,128]{1,0:T(8,128)S(1)}, f32[192,128]{1,0:T(8,128)S(1)},...) while((s32[]{:T(128)}, f32[32,16,128]{2,1,0:T(8,128)S(1)}, ...), condition=%wide.region_1.2_spmd.clone, body=%wide.region_0.1_spmd.sunk.clone | while | flops 1 | bytes 524457 | solution.py:859
  50.0 14.1 %all_to_all.12.arrived_ref = f32[32,16,128]{2,1,0:T(8,128)} all-to-all(f32[32,16,128]{2,1,0:T(8,128)S(1)} %get-tuple-element.384), channel_id=1, replica_groups=mesh['curve'=8,'slab'=4] {'curve','slab'}, dimensions={0} | all-to-all | bytes 524288 | tf_op jit(solution)/shard_map/while/body/all_to_all | solution.py:762
  64.0 18.3 %body.1 = (f32[32,16,128]{2,1,0:T(8,128)S(1)}, s32[1]{0:T(128)}, f32[288,128]{1,0:T(8,128)S(1)}, f32[288,128]{1,0:T(8,128)S(1)}, f32[192,128]{1,0:T(8,128)S(1)}, /*index=5*/f32[192,128]{1,0:T(8,128)S(1)}) custom-call(s32[1]{0:T(128)} %get-tuple-element.409.curve_ref, ...), custom_call_target="tpu_custom_call", output_to_operand_aliasing={{2}: (15, {}), {3}: (16, {}), {4}: (17, {}), {5}: (18, {})} | custom-call | tf_op jit(solution)/shard_map/while/body/pallas_call | solution.py:838
  83.0 13.6 %all_to_all.12.arrived_ref = f32[32,16,128]{2,1,0:T(8,128)} all-to-all(f32[32,16,128]{2,1,0:T(8,128)S(1)} %get-tuple-element.384), channel_id=1, replica_groups=mesh['curve'=8,'slab'=4] {'curve','slab'}, dimensions={0} | all-to-all | bytes 524288 | tf_op jit(solution)/shard_map/while/body/all_to_all | solution.py:762
  96.6 16.0 %body.1 = (f32[32,16,128]{2,1,0:T(8,128)S(1)}, s32[1]{0:T(128)}, f32[288,128]{1,0:T(8,128)S(1)}, f32[288,128]{1,0:T(8,128)S(1)}, f32[192,128]{1,0:T(8,128)S(1)}, /*index=5*/f32[192,128]{1,0:T(8,128)S(1)}) custom-call(s32[1]{0:T(128)} %get-tuple-element.409.curve_ref, ...), custom_call_target="tpu_custom_call", output_to_operand_aliasing={{2}: (15, {}), {3}: (16, {}), {4}: (17, {}), {5}: (18, {})} | custom-call | tf_op jit(solution)/shard_map/while/body/pallas_call | solution.py:838
  113.3 13.9 %all_to_all.12.arrived_ref = f32[32,16,128]{2,1,0:T(8,128)} all-to-all(f32[32,16,128]{2,1,0:T(8,128)S(1)} %get-tuple-element.384), channel_id=1, replica_groups=mesh['curve'=8,'slab'=4] {'curve','slab'}, dimensions={0} | all-to-all | bytes 524288 | tf_op jit(solution)/shard_map/while/body/all_to_all | solution.py:762
  127.2 13.7 %body.1 = (f32[32,16,128]{2,1,0:T(8,128)S(1)}, s32[1]{0:T(128)}, f32[288,128]{1,0:T(8,128)S(1)}, f32[288,128]{1,0:T(8,128)S(1)}, f32[192,128]{1,0:T(8,128)S(1)}, /*index=5*/f32[192,128]{1,0:T(8,128)S(1)}) custom-call(s32[1]{0:T(128)} %get-tuple-element.409.curve_ref, ...), custom_call_target="tpu_custom_call", output_to_operand_aliasing={{2}: (15, {}), {3}: (16, {}), {4}: (17, {}), {5}: (18, {})} | custom-call | tf_op jit(solution)/shard_map/while/body/pallas_call | solution.py:838
  141.6 14.6 %all_to_all.12.arrived_ref = f32[32,16,128]{2,1,0:T(8,128)} all-to-all(f32[32,16,128]{2,1,0:T(8,128)S(1)} %get-tuple-element.384), channel_id=1, replica_groups=mesh['curve'=8,'slab'=4] {'curve','slab'}, dimensions={0} | all-to-all | bytes 524288 | tf_op jit(solution)/shard_map/while/body/all_to_all | solution.py:762
  156.2 11.3 %body.1 = (f32[32,16,128]{2,1,0:T(8,128)S(1)}, s32[1]{0:T(128)}, f32[288,128]{1,0:T(8,128)S(1)}, f32[288,128]{1,0:T(8,128)S(1)}, f32[192,128]{1,0:T(8,128)S(1)}, /*index=5*/f32[192,128]{1,0:T(8,128)S(1)}) custom-call(s32[1]{0:T(128)} %get-tuple-element.409.curve_ref, ...), custom_call_target="tpu_custom_call", output_to_operand_aliasing={{2}: (15, {}), {3}: (16, {}), {4}: (17, {}), {5}: (18, {})} | custom-call | tf_op jit(solution)/shard_map/while/body/pallas_call | solution.py:838
  168.1 13.9 %all_to_all.12.arrived_ref = f32[32,16,128]{2,1,0:T(8,128)} all-to-all(f32[32,16,128]{2,1,0:T(8,128)S(1)} %get-tuple-element.384), channel_id=1, replica_groups=mesh['curve'=8,'slab'=4] {'curve','slab'}, dimensions={0} | all-to-all | bytes 524288 | tf_op jit(solution)/shard_map/while/body/all_to_all | solution.py:762
  182.1 7.2 %body.1 = (f32[32,16,128]{2,1,0:T(8,128)S(1)}, s32[1]{0:T(128)}, f32[288,128]{1,0:T(8,128)S(1)}, f32[288,128]{1,0:T(8,128)S(1)}, f32[192,128]{1,0:T(8,128)S(1)}, /*index=5*/f32[192,128]{1,0:T(8,128)S(1)}) custom-call(s32[1]{0:T(128)} %get-tuple-element.409.curve_ref, ...), custom_call_target="tpu_custom_call", output_to_operand_aliasing={{2}: (15, {}), {3}: (16, {}), {4}: (17, {}), {5}: (18, {})} | custom-call | tf_op jit(solution)/shard_map/while/body/pallas_call | solution.py:838
  190.0 16.8 %all_to_all.12.arrived_ref = f32[32,16,128]{2,1,0:T(8,128)} all-to-all(f32[32,16,128]{2,1,0:T(8,128)S(1)} %get-tuple-element.384), channel_id=1, replica_groups=mesh['curve'=8,'slab'=4] {'curve','slab'}, dimensions={0} | all-to-all | bytes 524288 | tf_op jit(solution)/shard_map/while/body/all_to_all | solution.py:762
  206.7 7.2 %body.1 = (f32[32,16,128]{2,1,0:T(8,128)S(1)}, s32[1]{0:T(128)}, f32[288,128]{1,0:T(8,128)S(1)}, f32[288,128]{1,0:T(8,128)S(1)}, f32[192,128]{1,0:T(8,128)S(1)}, /*index=5*/f32[192,128]{1,0:T(8,128)S(1)}) custom-call(s32[1]{0:T(128)} %get-tuple-element.409.curve_ref, ...), custom_call_target="tpu_custom_call", output_to_operand_aliasing={{2}: (15, {}), {3}: (16, {}), {4}: (17, {}), {5}: (18, {})} | custom-call | tf_op jit(solution)/shard_map/while/body/pallas_call | solution.py:838
  214.6 0.8 shard_map.124
  (6 shorter events, 0.2 us)
Async XLA Ops:
  0.6 49.3 %copy-start.1 = (bf16[288,384]{1,0:T(8,128)(2,1)S(1)}, bf16[288,384]{1,0:T(8,128)(2,1)}, u32[]{:S(2)}) copy-start(bf16[288,384]{1,0:T(8,128)(2,1)} %constant.25.clone..sunk.2) | copy-start | bytes 663556
  6.5 0.7 copy-start
  7.1 17.4 %all-to-all-start.1 = ((f32[32,16,128]{2,1,0:T(8,128)}), f32[32,16,128]{2,1,0:T(8,128)S(1)}, u32[]{:S(2)}, u32[]{:S(2)}) async-start(f32[32,16,128]{2,1,0:T(8,128)} %get-tuple-element.134), calls=%async_computation.1 | async-start | bytes 524288 | tf_op jit(solution)/shard_map/all_to_all | solution.py:762
  24.6 0.7 copy-start.2
where the time goes:
time: 219 us; the launch traced here: 215 us
  Pallas kernels  102 us (47%)
  blocking collectives  86.8 us (40%)
  waiting for transfers between devices  10.3 us (5%)
  starting transfers between devices  7.1 us (3%)
  loops' own time  3.97 us (2%)
  local copies, waits for them, and re-layouts  3.18 us (1%)
    all_to_all x6, blocking collectives, exchange(): return lax.all_to_all(message, ('curve', 'slab'), 0, 0, tiled=True)  86.8 us
    pallas_call x6, Pallas kernels, one_round(): round_call(curve, span, exchange(message), ints, floats, sends, near, wei...  73.8 us
    pallas_call x1, Pallas kernels, body(): call(functools.partial(first_kernel, z), [shape(z.devices, 16, n), kept(z...  24.7 us
    all_to_all x1, waiting for transfers between devices, exchange(): return lax.all_to_all(message, ('curve', 'slab'), 0, 0, tiled=True)  10.3 us
    all_to_all x1, starting transfers between devices, exchange(): return lax.all_to_all(message, ('curve', 'slab'), 0, 0, tiled=True)  7.1 us
  transfers between devices with their start and end apart: 1, of which 1 were waited for; matrix products, arithmetic and copies ran while one was open for 0% of the time, Pallas kernels for 0%

commit v1 on v0

--- a/solution.py
+++ b/solution.py
@@ -196,6 +196,8 @@
         span_ref[level] = before // z.width
         span_ref[z.levels + level] = jnp.where(upto > before, (upto + z.width - 1) // z.width, before // z.width)
 
+    span_ref[2 * z.levels] = 1
+
     link = jnp.concatenate([link_ref[...], jnp.full((SUB - FACES, n), -1, jnp.int32)], axis=0)
     near = jnp.where(link >= 0, lane_take(pos, jnp.maximum(link, 0)), -1)
     near = lane_take(near, perm)
@@ -384,7 +386,8 @@
     stack_ref,
     part_ref,
     fresh_ref,
-    fetches,
+    fetch=None,
+    open_ref=None,
 ):
     n = z.columns
     near = ints_ref[3]
@@ -422,10 +425,40 @@
                 scale = jnp.where(chunk_of == half * per_sum + at_chunk, float((2 * z.width) ** at_chunk), scale)
             counts.append(jnp.sum(fresh * scale).astype(jnp.int32))
 
-    for fetch in fetches:
-        fetch.wait()
+    shift = (2 * z.width).bit_length() - 1
+
+    def count_of(chunk, backward):
+        low, high = counts[2 * backward], counts[2 * backward + 1]
+        bits = jnp.where(chunk >= per_sum, high, low)
+        bits = lax.shift_right_logical(bits, lax.rem(chunk, per_sum) * shift)
+        return jnp.bitwise_and(bits, 2 * z.width - 1)
+
+    def fetch_for(chunk, backward):
+        needed = count_of(chunk, backward) > 0
+        if backward:
+            needed &= open_ref[chunk] == 0
+
+        @pl.when(needed)
+        def _():
+            fetch(chunk).start()
+            open_ref[chunk] = 1
+
+    if fetch is not None:
+        for chunk in range(GROUPS):
+            open_ref[chunk] = 0
+        for chunk in range(GROUPS):
+            fetch_for(jnp.int32(chunk), False)
+        for chunk in reversed(range(GROUPS)):
+            fetch_for(jnp.int32(chunk), True)
 
     def step(level, chunk, backward):
+        if fetch is not None:
+
+            @pl.when(open_ref[chunk] == 1)
+            def _():
+                fetch(chunk).wait()
+                open_ref[chunk] = 2
+
         old = forward_table_ref
         new = swept_table_ref
         base = swept_base if backward else forward_base
@@ -457,17 +490,12 @@
         out_table[...] = jnp.where(keep, table, out_table[...])
 
     for backward in (False, True):
-        low, high = counts[2 * backward], counts[2 * backward + 1]
-
-        def run(count, carry, backward=backward, low=low, high=high):
+
+        def run(count, carry, backward=backward):
             level = z.levels - 1 - count if backward else count
 
             def one(chunk, inner):
-                bits = jnp.where(chunk >= per_sum, high, low)
-                shift = (2 * z.width).bit_length() - 1
-                bits = lax.shift_right_logical(bits, lax.rem(chunk, per_sum) * shift)
-
-                @pl.when(jnp.bitwise_and(bits, 2 * z.width - 1) > 0)
+                @pl.when(count_of(chunk, backward) > 0)
                 def _():
                     step(level, chunk, backward)
 
@@ -581,7 +609,6 @@
         stack_ref,
         part_ref,
         fresh_ref,
-        (),
     )
     send_messages(z, curve, sends_ref, kinds_ref, forward_table_ref, swept_table_ref, message_ref)
     for ii in range(z.rows):
@@ -623,14 +650,14 @@
     swept_base_ref,
     chunks_ref,
     sems,
+    open_ref,
 ):
     n = z.columns
     curve = curve_ref[0]
-    fetches = [
-        pltpu.make_async_copy(chunks_in.at[chunk], chunks_ref.at[chunk], sems.at[chunk]) for chunk in range(GROUPS)
-    ]
-    for fetch in fetches:
-        fetch.start()
+
+    def fetch(chunk):
+        return pltpu.make_async_copy(chunks_in.at[chunk], chunks_ref.at[chunk], sems.at[chunk])
+
     forward_table_ref[...] = forward_table_in[...]
     swept_table_ref[...] = swept_table_in[...]
     forward_ref[...] = forward_in[...]
@@ -668,7 +695,8 @@
         stack_ref,
         part_ref,
         fresh_ref,
-        fetches,
+        fetch,
+        open_ref,
     )
     send_messages(z, curve, sends_ref, kinds_ref, forward_table_ref, swept_table_ref, message_ref)
 
@@ -746,7 +774,7 @@
             kept(5, SUB, n, kind=jnp.int32),
             kept(7, SUB, n),
             kept(3, SUB, n, kind=jnp.int32),
-            shape(2 * levels, kind=jnp.int32),
+            shape(2 * levels + 1, kind=jnp.int32),
             kept(z.table_rows, n),
             shape(z.devices, 16, n),
         ],
@@ -798,7 +826,7 @@
         smem_in=(0, 1),
         hbm_in=(11,),
         hbm_out=(5,),
-        vmem=56,
+        vmem=48,
     )(
         curve,
         span,
@@ -825,9 +853,10 @@
             pltpu.VMEM((z.block_pad, n), F32),
             pltpu.VMEM((GROUPS, z.rows, z.block_pad, n), F32),
             pltpu.SemaphoreType.DMA((GROUPS,)),
+            pltpu.SMEM((GROUPS,), jnp.int32),
         ],
         hbm_in=(10,),
-        vmem=56,
+        vmem=16,
         aliases={15: 2, 16: 3, 17: 4, 18: 5},
         smem_in=(0, 1),
         smem_out=(1,),

time: 219 us -> 244 us (1.11)
  blocking collectives: 86.8 us -> 128 us
  Pallas kernels: 102 us -> 85.3 us
    all_to_all x6 -> x8, blocking collectives: 86.8 us -> 128 us  [exchange(): return lax.all_to_all(message, ('curve', 'slab'), 0, 0, tiled=True)]
    pallas_call x6 -> x8, Pallas kernels: 73.8 us -> 62.2 us  [one_round(): round_call(curve, span, exchange(message), ints, floats, sends, near, wei...]
    pallas_call x1, Pallas kernels: 24.7 us -> 19.3 us  [body(): call(functools.partial(first_kernel, z), [shape(z.devices, 16, n), kept(z...]
where the time goes in v1:
time: 244 us; the launch traced here: 241 us
  blocking collectives  128 us (52%)
  Pallas kernels  85.3 us (35%)
  waiting for transfers between devices  10.3 us (4%)
  starting transfers between devices  7.1 us (3%)
  loops' own time  5.29 us (2%)
  local copies, waits for them, and re-layouts  4.31 us (2%)
    all_to_all x8, blocking collectives, exchange(): return lax.all_to_all(message, ('curve', 'slab'), 0, 0, tiled=True)  128 us
    pallas_call x8, Pallas kernels, one_round(): round_call(curve, span, exchange(message), ints, floats, sends, near, wei...  62.2 us
    pallas_call x1, Pallas kernels, body(): call(functools.partial(first_kernel, z), [shape(z.devices, 16, n), kept(z...  19.3 us
    all_to_all x1, waiting for transfers between devices, exchange(): return lax.all_to_all(message, ('curve', 'slab'), 0, 0, tiled=True)  10.3 us
    all_to_all x1, starting transfers between devices, exchange(): return lax.all_to_all(message, ('curve', 'slab'), 0, 0, tiled=True)  7.1 us
    another operation x1, loops' own time, body(): _, _, state = lax.while_loop(lambda carry: carry[0] > 0, one_round, start)  5.29 us
  transfers between devices with their start and end apart: 1, of which 1 were waited for; matrix products, arithmetic and copies ran while one was open for 0% of the time, Pallas kernels for 0%

profile of v1, /device:TPU:1, one launch (start us, length us, event | category | flops | bytes accessed | tf_op | source)
XLA Modules:
  0.0 241.5 jit_solution(17540097890415236384)
XLA Ops:
  0.6 1.0 pad.9
  3.4 3.1 %shard_map.122 = (s32[5,8,128]{2,1,0:T(8,128)S(1)}, f32[7,8,128]{2,1,0:T(8,128)S(1)}, s32[3,8,128]{2,1,0:T(8,128)S(1)}, s32[17]{0:T(128)S(1)}, f32[288,128]{1,0:T(8,128)S(1)}, /*index=5*/f32[32,16,128]{2,1,0:T(8,128)}) custom-call(s32[1]{0:T(128)} %bitcast.curve_ref, f32[135,128]{1,0:T(8,128)} %start_ref.1, s32[1,128]{1,0:T(1,128)} %bitcast.8, ...), custom_call_target="tpu_custom_call" | custom-call | tf_op jit(solution)/shard_map/pallas_call | solution.py:771
  6.5 7.1 %all-to-all-start.1 = ((f32[32,16,128]{2,1,0:T(8,128)}), f32[32,16,128]{2,1,0:T(8,128)S(1)}, u32[]{:S(2)}, u32[]{:S(2)}) async-start(f32[32,16,128]{2,1,0:T(8,128)} %get-tuple-element.134), calls=%async_computation.1 | async-start | bytes 524288 | tf_op jit(solution)/shard_map/all_to_all | solution.py:790
  13.6 10.3 %all-to-all-done.1.arrived_ref = f32[32,16,128]{2,1,0:T(8,128)S(1)} async-done(((f32[32,16,128]{2,1,0:T(8,128)}), f32[32,16,128]{2,1,0:T(8,128)S(1)}, u32[]{:S(2)}, u32[]{:S(2)}) %all-to-all-start.1) | async-done | bytes 262176 | tf_op jit(solution)/shard_map/all_to_all | solution.py:790
  23.9 0.9 copy-done
  24.9 0.9 copy-done.1
  26.4 19.3 %shard_map.123 = (f32[32,16,128]{2,1,0:T(8,128)S(1)}, f32[136,128]{1,0:T(8,128)S(1)}, f32[136,128]{1,0:T(8,128)S(1)}, f32[3,48,128]{2,1,0:T(8,128)S(1)}, s32[3,1...) custom-call(s32[1]{0:T(128)} %bitcast.curve_ref, ...), custom_call_target="tpu_custom_call" | custom-call | tf_op jit(solution)/shard_map/pallas_call | solution.py:805
  45.7 195.0 %while.19 = (s32[]{:T(128)}, f32[32,16,128]{2,1,0:T(8,128)S(1)}, f32[288,128]{1,0:T(8,128)S(1)}, f32[288,128]{1,0:T(8,128)S(1)}, f32[192,128]{1,0:T(8,128)S(1)},...) while((s32[]{:T(128)}, f32[32,16,128]{2,1,0:T(8,128)S(1)}, ...), condition=%wide.region_1.2_spmd.clone, body=%wide.region_0.1_spmd.sunk.clone | while | flops 1 | bytes 524457 | solution.py:888
  45.7 18.4 %all_to_all.12.arrived_ref = f32[32,16,128]{2,1,0:T(8,128)S(1)} all-to-all(f32[32,16,128]{2,1,0:T(8,128)S(1)} %get-tuple-element.384), channel_id=1, replica_groups=mesh['curve'=8,'slab'=4] {'curve','slab'}, dimensions={0} | all-to-all | bytes 524288 | tf_op jit(solution)/shard_map/while/body/all_to_all | solution.py:790
  64.1 16.5 %body.1 = (f32[32,16,128]{2,1,0:T(8,128)S(1)}, s32[1]{0:T(128)}, f32[288,128]{1,0:T(8,128)S(1)}, f32[288,128]{1,0:T(8,128)S(1)}, f32[192,128]{1,0:T(8,128)S(1)}, /*index=5*/f32[192,128]{1,0:T(8,128)S(1)}) custom-call(s32[1]{0:T(128)} %get-tuple-element.409.curve_ref, ...), custom_call_target="tpu_custom_call", output_to_operand_aliasing={{2}: (15, {}), {3}: (16, {}), {4}: (17, {}), {5}: (18, {})} | custom-call | tf_op jit(solution)/shard_map/while/body/pallas_call | solution.py:867
  81.3 12.7 %all_to_all.12.arrived_ref = f32[32,16,128]{2,1,0:T(8,128)S(1)} all-to-all(f32[32,16,128]{2,1,0:T(8,128)S(1)} %get-tuple-element.384), channel_id=1, replica_groups=mesh['curve'=8,'slab'=4] {'curve','slab'}, dimensions={0} | all-to-all | bytes 524288 | tf_op jit(solution)/shard_map/while/body/all_to_all | solution.py:790
  94.0 14.2 %body.1 = (f32[32,16,128]{2,1,0:T(8,128)S(1)}, s32[1]{0:T(128)}, f32[288,128]{1,0:T(8,128)S(1)}, f32[288,128]{1,0:T(8,128)S(1)}, f32[192,128]{1,0:T(8,128)S(1)}, /*index=5*/f32[192,128]{1,0:T(8,128)S(1)}) custom-call(s32[1]{0:T(128)} %get-tuple-element.409.curve_ref, ...), custom_call_target="tpu_custom_call", output_to_operand_aliasing={{2}: (15, {}), {3}: (16, {}), {4}: (17, {}), {5}: (18, {})} | custom-call | tf_op jit(solution)/shard_map/while/body/pallas_call | solution.py:867
  108.9 13.5 %all_to_all.12.arrived_ref = f32[32,16,128]{2,1,0:T(8,128)S(1)} all-to-all(f32[32,16,128]{2,1,0:T(8,128)S(1)} %get-tuple-element.384), channel_id=1, replica_groups=mesh['curve'=8,'slab'=4] {'curve','slab'}, dimensions={0} | all-to-all | bytes 524288 | tf_op jit(solution)/shard_map/while/body/all_to_all | solution.py:790
  122.4 10.3 %body.1 = (f32[32,16,128]{2,1,0:T(8,128)S(1)}, s32[1]{0:T(128)}, f32[288,128]{1,0:T(8,128)S(1)}, f32[288,128]{1,0:T(8,128)S(1)}, f32[192,128]{1,0:T(8,128)S(1)}, /*index=5*/f32[192,128]{1,0:T(8,128)S(1)}) custom-call(s32[1]{0:T(128)} %get-tuple-element.409.curve_ref, ...), custom_call_target="tpu_custom_call", output_to_operand_aliasing={{2}: (15, {}), {3}: (16, {}), {4}: (17, {}), {5}: (18, {})} | custom-call | tf_op jit(solution)/shard_map/while/body/pallas_call | solution.py:867
  133.4 15.7 %all_to_all.12.arrived_ref = f32[32,16,128]{2,1,0:T(8,128)S(1)} all-to-all(f32[32,16,128]{2,1,0:T(8,128)S(1)} %get-tuple-element.384), channel_id=1, replica_groups=mesh['curve'=8,'slab'=4] {'curve','slab'}, dimensions={0} | all-to-all | bytes 524288 | tf_op jit(solution)/shard_map/while/body/all_to_all | solution.py:790
  149.1 6.2 %body.1 = (f32[32,16,128]{2,1,0:T(8,128)S(1)}, s32[1]{0:T(128)}, f32[288,128]{1,0:T(8,128)S(1)}, f32[288,128]{1,0:T(8,128)S(1)}, f32[192,128]{1,0:T(8,128)S(1)}, /*index=5*/f32[192,128]{1,0:T(8,128)S(1)}) custom-call(s32[1]{0:T(128)} %get-tuple-element.409.curve_ref, ...), custom_call_target="tpu_custom_call", output_to_operand_aliasing={{2}: (15, {}), {3}: (16, {}), {4}: (17, {}), {5}: (18, {})} | custom-call | tf_op jit(solution)/shard_map/while/body/pallas_call | solution.py:867
  155.9 17.6 %all_to_all.12.arrived_ref = f32[32,16,128]{2,1,0:T(8,128)S(1)} all-to-all(f32[32,16,128]{2,1,0:T(8,128)S(1)} %get-tuple-element.384), channel_id=1, replica_groups=mesh['curve'=8,'slab'=4] {'curve','slab'}, dimensions={0} | all-to-all | bytes 524288 | tf_op jit(solution)/shard_map/while/body/all_to_all | solution.py:790
  173.6 3.7 %body.1 = (f32[32,16,128]{2,1,0:T(8,128)S(1)}, s32[1]{0:T(128)}, f32[288,128]{1,0:T(8,128)S(1)}, f32[288,128]{1,0:T(8,128)S(1)}, f32[192,128]{1,0:T(8,128)S(1)}, /*index=5*/f32[192,128]{1,0:T(8,128)S(1)}) custom-call(s32[1]{0:T(128)} %get-tuple-element.409.curve_ref, ...), custom_call_target="tpu_custom_call", output_to_operand_aliasing={{2}: (15, {}), {3}: (16, {}), {4}: (17, {}), {5}: (18, {})} | custom-call | tf_op jit(solution)/shard_map/while/body/pallas_call | solution.py:867
  178.0 17.6 %all_to_all.12.arrived_ref = f32[32,16,128]{2,1,0:T(8,128)S(1)} all-to-all(f32[32,16,128]{2,1,0:T(8,128)S(1)} %get-tuple-element.384), channel_id=1, replica_groups=mesh['curve'=8,'slab'=4] {'curve','slab'}, dimensions={0} | all-to-all | bytes 524288 | tf_op jit(solution)/shard_map/while/body/all_to_all | solution.py:790
  195.6 3.7 %body.1 = (f32[32,16,128]{2,1,0:T(8,128)S(1)}, s32[1]{0:T(128)}, f32[288,128]{1,0:T(8,128)S(1)}, f32[288,128]{1,0:T(8,128)S(1)}, f32[192,128]{1,0:T(8,128)S(1)}, /*index=5*/f32[192,128]{1,0:T(8,128)S(1)}) custom-call(s32[1]{0:T(128)} %get-tuple-element.409.curve_ref, ...), custom_call_target="tpu_custom_call", output_to_operand_aliasing={{2}: (15, {}), {3}: (16, {}), {4}: (17, {}), {5}: (18, {})} | custom-call | tf_op jit(solution)/shard_map/while/body/pallas_call | solution.py:867
  200.0 16.9 %all_to_all.12.arrived_ref = f32[32,16,128]{2,1,0:T(8,128)S(1)} all-to-all(f32[32,16,128]{2,1,0:T(8,128)S(1)} %get-tuple-element.384), channel_id=1, replica_groups=mesh['curve'=8,'slab'=4] {'curve','slab'}, dimensions={0} | all-to-all | bytes 524288 | tf_op jit(solution)/shard_map/while/body/all_to_all | solution.py:790
  216.9 3.7 %body.1 = (f32[32,16,128]{2,1,0:T(8,128)S(1)}, s32[1]{0:T(128)}, f32[288,128]{1,0:T(8,128)S(1)}, f32[288,128]{1,0:T(8,128)S(1)}, f32[192,128]{1,0:T(8,128)S(1)}, /*index=5*/f32[192,128]{1,0:T(8,128)S(1)}) custom-call(s32[1]{0:T(128)} %get-tuple-element.409.curve_ref, ...), custom_call_target="tpu_custom_call", output_to_operand_aliasing={{2}: (15, {}), {3}: (16, {}), {4}: (17, {}), {5}: (18, {})} | custom-call | tf_op jit(solution)/shard_map/while/body/pallas_call | solution.py:867
  221.3 15.0 %all_to_all.12.arrived_ref = f32[32,16,128]{2,1,0:T(8,128)S(1)} all-to-all(f32[32,16,128]{2,1,0:T(8,128)S(1)} %get-tuple-element.384), channel_id=1, replica_groups=mesh['curve'=8,'slab'=4] {'curve','slab'}, dimensions={0} | all-to-all | bytes 524288 | tf_op jit(solution)/shard_map/while/body/all_to_all | solution.py:790
  236.3 3.7 %body.1 = (f32[32,16,128]{2,1,0:T(8,128)S(1)}, s32[1]{0:T(128)}, f32[288,128]{1,0:T(8,128)S(1)}, f32[288,128]{1,0:T(8,128)S(1)}, f32[192,128]{1,0:T(8,128)S(1)}, /*index=5*/f32[192,128]{1,0:T(8,128)S(1)}) custom-call(s32[1]{0:T(128)} %get-tuple-element.409.curve_ref, ...), custom_call_target="tpu_custom_call", output_to_operand_aliasing={{2}: (15, {}), {3}: (16, {}), {4}: (17, {}), {5}: (18, {})} | custom-call | tf_op jit(solution)/shard_map/while/body/pallas_call | solution.py:867
  (12 shorter events, 3.1 us)
Async XLA Ops:
  0.6 45.1 %copy-start.3 = (bf16[288,384]{1,0:T(8,128)(2,1)S(1)}, bf16[288,384]{1,0:T(8,128)(2,1)}, u32[]{:S(2)}) copy-start(bf16[288,384]{1,0:T(8,128)(2,1)} %constant.25.clone..sunk.2) | copy-start | bytes 663556
  6.5 17.5 %all-to-all-start.1 = ((f32[32,16,128]{2,1,0:T(8,128)}), f32[32,16,128]{2,1,0:T(8,128)S(1)}, u32[]{:S(2)}, u32[]{:S(2)}) async-start(f32[32,16,128]{2,1,0:T(8,128)} %get-tuple-element.134), calls=%async_computation.1 | async-start | bytes 524288 | tf_op jit(solution)/shard_map/all_to_all | solution.py:790
  23.9 0.9 copy-start
  24.9 0.9 copy-start.1
  25.8 0.7 copy-start.2
